TPU v7x, 32 devices: a whole 2x2x4 slice. The times are simulated.
32 devices in a mesh: runs: 2 (over x), patch: 16 (over z, y, core).
Axes of the slice: x: 2, y: 2, z: 4, core: 2. Of those that a mesh axis runs over, the one named last changes fastest.
Arguments:
- depths: float32 [2, 128, 4096], P(None, None, ('runs', 'patch')), parts along dimension 2, may hold values from 0.4 to 1.6
- momenta: float32 [4, 128, 4096], P(None, None, ('runs', 'patch')), parts along dimension 2, may hold values from -1 to 1
- bed: float32 [128, 4096], P(None, ('runs', 'patch')), parts along dimension 1, may hold values from -3 to 3
- active: int32 [1, 32], P(None, ('runs', 'patch')), parts along dimension 1, may hold values from 0 to 1
Outputs:
- new_depths: float32 [2, 128, 4096], P(None, None, ('runs', 'patch')), parts along dimension 2
- new_momenta: float32 [4, 128, 4096], P(None, None, ('runs', 'patch')), parts along dimension 2
There are 2 independent parts, one for each index of `runs`. A program takes and returns all parts, laid end to end along the dimension named above; each array names one. Nothing has to cross between parts.
All inputs are finite; a program needn't handle non-finite values.
Results may differ from a plain program's by a relative error of at most 0.0003.
Values sent between devices are 32-bit elements; how exact they have to be, the bound alone decides.
A program may use at most 64 MiB of HBM per device.

v0:
```python
import functools

import jax
import jax.numpy as jnp
from jax import lax
from jax.experimental import pallas as pl
from jax.experimental.pallas import tpu as pltpu
from jax.sharding import PartitionSpec as P

time_step = 0.04
solid_press = 0.6
fluid_press = 1.0
drag_coef = 0.5
friction_coef = 0.2
velocity_eps = 0.01
depth_eps = 0.0001
spread_eps = 1e-06
halo = 6
core_cols = 2 * halo
strip = 3 * halo
pair = 2 * strip
segments = 3
tiny = 1e-30

MESH = pl.DeviceIdType.MESH


def recip(x):
    return pl.reciprocal(x, approx=True)


def lanes(x, shift):
    shift = shift % x.shape[-1]
    return x if shift == 0 else pltpu.roll(x, shift, 1)


def minmod(a, b):
    return jnp.maximum(jnp.minimum(a, b), jnp.minimum(jnp.maximum(a, b), 0.0))


def wave(depth, pressure):
    x = pressure * depth
    return jnp.maximum(x, 0.0) * lax.rsqrt(jnp.maximum(x, tiny))


def hll(left, right, pressure):
    hl, ml, tl = left
    hr, mr, tr = right
    hl2 = hl * hl
    hr2 = hr * hr
    ul = ml * hl * recip(hl2 + depth_eps)
    ur = mr * hr * recip(hr2 + depth_eps)
    cl = wave(hl, pressure)
    cr = wave(hr, pressure)
    low = jnp.minimum(jnp.minimum(ul - cl, ur - cr), 0.0)
    high = jnp.maximum(jnp.maximum(ul + cl, ur + cr), 0.0)
    r = time_step * recip(high - low + spread_eps)
    a = high * r
    b = low * r
    c = a * low
    al = a * ul - c
    br = b * ur - c
    fh = a * ml - b * mr + c * (hr - hl)
    fn = al * ml - br * mr + (0.5 * pressure) * (a * hl2 - b * hr2)
    ft = al * tl - br * tr
    return fh, fn, ft


def both_phases(left, right, offset):
    out = [None] * 6
    for phase, pressure in ((0, solid_press), (1, fluid_press)):
        ids = (phase, 2 + 2 * phase + offset, 3 + 2 * phase - offset)
        parts = hll([left[i] for i in ids], [right[i] for i in ids], pressure)
        for i, part in zip(ids, parts):
            out[i] = part
    return out


def row_states(src, at):
    lefts, rights = [], []
    for f in range(6):
        v = src[f, pl.ds(at, 8), :]
        below = src[f, pl.ds(at - 1, 8), :]
        above = src[f, pl.ds(at + 1, 8), :]
        s = 0.5 * minmod(v - below, above - v)
        lefts.append(v + s)
        rights.append(v - s)
    return lefts, rights


def tendency(v, br, bc):
    lefts, rights = [], []
    for f in range(6):
        h = 0.5 * v[f]
        d = h - lanes(h, 1)
        s = minmod(d, lanes(d, -1))
        lefts.append(lanes(v[f] + s, 1))
        rights.append(v[f] - s)
    flux = both_phases(lefts, rights, 1)
    change = [lanes(x, -1) - x for x in flux]
    hs, hf = v[0], v[1]
    ws = hs * recip(hs * hs + depth_eps)
    wf = hf * recip(hf * hf + depth_eps)
    sr, sc, fr, fc = v[2] * ws, v[3] * ws, v[4] * wf, v[5] * wf
    drag = (time_step * drag_coef) * hs * hf * recip(jnp.abs(hs) + jnp.abs(hf) + depth_eps)
    rub = (time_step * friction_coef) * hs * lax.rsqrt(sr * sr + sc * sc + velocity_eps)
    dr = drag * (fr - sr)
    dc = drag * (fc - sc)
    ps = solid_press * hs
    pf = fluid_press * hf
    gains = [
        None,
        None,
        dr - ps * br - rub * sr,
        dc - ps * bc - rub * sc,
        dr + pf * br,
        dc + pf * bc,
    ]
    out = []
    for f in range(6):
        if f < 2:
            out.append(-change[f])
        elif f < 4:
            out.append(gains[f] - change[f])
        else:
            out.append(-gains[f] - change[f])
    return out


def run_stage(stage, src, start, beds, dst, first, count, unroll):
    row = lax.broadcasted_iota(jnp.int32, (8, 128), 0)
    top = row == 0
    bottom = row == 7

    def faces(at, carried):
        lefts, rights = row_states(src, at)
        rolled = [pltpu.roll(x, 1, 0) for x in lefts]
        shifted = [jnp.where(top, a, b) for a, b in zip(carried, rolled)]
        return both_phases(shifted, rights, 0), rolled

    at0 = first * 8
    lefts, _ = row_states(src, max(at0 - 8, 8))
    carried = [pltpu.roll(x, 1, 0) for x in lefts]
    flux, carried = faces(at0, carried)
    rolled_flux = [pltpu.roll(x, 7, 0) for x in flux]

    def one(at, carried, flux, rolled_flux):
        nxt, carried = faces(at + 8, carried)
        rolled_next = [pltpu.roll(x, 7, 0) for x in nxt]
        v = [src[f, pl.ds(at, 8), :] for f in range(6)]
        gain = tendency(v, beds[0, pl.ds(at, 8), :], beds[1, pl.ds(at, 8), :])
        for f in range(6):
            up = jnp.where(bottom, rolled_next[f], rolled_flux[f])
            new = v[f] + (gain[f] - (up - flux[f]))
            if stage == 1:
                new = 0.75 * start[f, pl.ds(at, 8), :] + 0.25 * new
            elif stage == 2:
                new = (1.0 / 3.0) * start[f, pl.ds(at, 8), :] + (2.0 / 3.0) * new
            dst[f, pl.ds(at, 8), :] = new
        return carried, nxt, rolled_next

    def body(i, state):
        carried, flux, rolled_flux = state
        base = pl.multiple_of(at0 + i * (8 * unroll), 8)
        for u in range(unroll):
            carried, flux, rolled_flux = one(base + 8 * u, carried, flux, rolled_flux)
        return carried, flux, rolled_flux

    lax.fori_loop(0, count // unroll, body, (carried, flux, rolled_flux))


def bed_slopes(x, beds, first, count):
    def body(i, carry):
        at = pl.multiple_of((first + i) * 8, 8)
        b = x[6, pl.ds(at, 8), :]
        beds[0, pl.ds(at, 8), :] = (0.5 * time_step) * (
            x[6, pl.ds(at + 1, 8), :] - x[6, pl.ds(at - 1, 8), :]
        )
        beds[1, pl.ds(at, 8), :] = (0.5 * time_step) * (lanes(b, -1) - lanes(b, 1))
        return carry

    lax.fori_loop(0, count, body, 0)


def kernel(count, rows, depths, momenta, bed, active, out_d, out_m,
           x, beds, one, two, sx, sbeds, sone, stwo, send, recv, send_sem, recv_sem):
    me = lax.axis_index("patch")
    right, left = lax.rem(me + 1, count), lax.rem(me + count - 1, count)
    barrier = pltpu.get_barrier_semaphore()
    for other in (left, right):
        pl.semaphore_signal(barrier, inc=1, device_id={"patch": other}, device_id_type=MESH)

    lane = lax.broadcasted_iota(jnp.int32, (8, 128), 1)
    groups = rows // 8
    step = 40
    strip_groups = 8
    end = 16 + rows

    for f in range(7):
        own = depths.at[f] if f < 2 else momenta.at[f - 2] if f < 6 else bed
        x[f, 16:end, :] = own[...]
        x[f, 0:16, :] = jnp.broadcast_to(own[0:1, :], (16, 128))
        x[f, end : end + 24, :] = jnp.broadcast_to(own[rows - 1 : rows, :], (24, 128))

    def pack(q, carry):
        to_left = jnp.zeros((8, 128), jnp.float32)
        to_right = jnp.zeros((8, 128), jnp.float32)
        for f in range(7):
            for s in range(segments):
                v = x[f, pl.ds(pl.multiple_of(8 + step * s + 8 * q, 8), 8), :]
                at = strip * f + halo * s
                here = (lane >= at) & (lane < at + halo)
                to_left = jnp.where(here, lanes(v, at), to_left)
                to_right = jnp.where(here, lanes(v, at - (128 - halo)), to_right)
        rows_q = pl.ds(pl.multiple_of(8 * q, 8), 8)
        send[0, rows_q, :] = to_left
        send[1, rows_q, :] = to_right
        return carry

    lax.fori_loop(0, strip_groups, pack, 0)

    pl.semaphore_wait(barrier, 2)
    copies = []
    for i, other in ((0, left), (1, right)):
        copy = pltpu.make_async_remote_copy(
            src_ref=send.at[i],
            dst_ref=recv.at[i],
            send_sem=send_sem.at[i],
            recv_sem=recv_sem.at[i],
            device_id={"patch": other},
            device_id_type=MESH,
        )
        copy.start()
        copies.append(copy)

    bed_slopes(x, beds, 1, groups + 2)
    run_stage(0, x, x, beds, one, 1, groups + 2, 2)
    run_stage(1, one, x, beds, two, 1, groups + 2, 2)
    run_stage(2, two, x, beds, one, 2, groups, 2)

    for copy in copies:
        copy.wait()

    def gather(q, carry):
        rows_q = pl.ds(pl.multiple_of(8 * q, 8), 8)
        from_right = recv[0, rows_q, :]
        from_left = recv[1, rows_q, :]
        dest = pl.ds(pl.multiple_of(8 + 8 * q, 8), 8)
        for f in range(7):
            acc = jnp.zeros((8, 128), jnp.float32)
            for s in range(segments):
                v = x[f, pl.ds(pl.multiple_of(8 + step * s + 8 * q, 8), 8), :]
                at = strip * f + halo * s
                base = pair * s
                pieces = (
                    (lanes(v, base - (128 - core_cols)), base, core_cols),
                    (lanes(from_right, base + core_cols - at), base + core_cols, halo),
                    (lanes(from_left, base + strip - at), base + strip, halo),
                    (lanes(v, base + strip + halo), base + strip + halo, core_cols),
                )
                for moved, begin, width in pieces:
                    acc = jnp.where((lane >= begin) & (lane < begin + width), moved, acc)
            sx[f, dest, :] = acc
        return carry

    lax.fori_loop(0, strip_groups, gather, 0)
    for f in range(7):
        sx[f, 0:8, :] = sx[f, 8:16, :]
        sx[f, 72:88, :] = sx[f, 56:72, :]

    bed_slopes(sx, sbeds, 1, strip_groups)
    run_stage(0, sx, sx, sbeds, sone, 1, strip_groups, 2)
    run_stage(1, sone, sx, sbeds, stwo, 1, strip_groups, 2)
    run_stage(2, stwo, sx, sbeds, sone, 2, strip_groups - 2, 2)

    live = jnp.broadcast_to(active[...], (8, 128)) > 0
    left_edge = lane < halo
    right_edge = lane >= 128 - halo

    def merge(s, begin):
        def body(q, carry):
            strip_at = pl.multiple_of(8 * q, 8)
            row_at = pl.multiple_of(8 * q + (step * s - 16), 8)
            for f in range(6):
                e = sone[f, pl.ds(strip_at, 8), :]
                new = one[f, pl.ds(row_at + 16, 8), :]
                new = jnp.where(left_edge, lanes(e, -(pair * s + strip + halo)), new)
                new = jnp.where(right_edge, lanes(e, 128 - halo - (pair * s + halo)), new)
                new = jnp.where(live, new, x[f, pl.ds(row_at + 16, 8), :])
                if f < 2:
                    out_d[f, pl.ds(row_at, 8), :] = new
                else:
                    out_m[f - 2, pl.ds(row_at, 8), :] = new
            return carry

        lax.fori_loop(begin, strip_groups, body, 0)

    merge(0, 2)
    merge(1, 3)
    merge(2, 3)


def per_device(depths, momenta, bed, active):
    rows, cols = bed.shape
    count = lax.axis_size("patch")
    tall = rows + 40
    f32 = jnp.float32
    vmem = pl.BlockSpec(memory_space=pltpu.VMEM)
    return pl.pallas_call(
        functools.partial(kernel, count, rows),
        out_shape=(
            jax.ShapeDtypeStruct(depths.shape, f32),
            jax.ShapeDtypeStruct(momenta.shape, f32),
        ),
        in_specs=[vmem] * 4,
        out_specs=(vmem, vmem),
        scratch_shapes=[
            pltpu.VMEM((7, tall, cols), f32),
            pltpu.VMEM((2, tall, cols), f32),
            pltpu.VMEM((6, tall, cols), f32),
            pltpu.VMEM((6, tall, cols), f32),
            pltpu.VMEM((7, 88, cols), f32),
            pltpu.VMEM((2, 88, cols), f32),
            pltpu.VMEM((6, 88, cols), f32),
            pltpu.VMEM((6, 88, cols), f32),
            pltpu.VMEM((2, 64, cols), f32),
            pltpu.VMEM((2, 64, cols), f32),
            pltpu.SemaphoreType.DMA((2,)),
            pltpu.SemaphoreType.DMA((2,)),
        ],
        compiler_params=pltpu.CompilerParams(
            collective_id=0, has_side_effects=True, vmem_limit_bytes=32 * 1024 * 1024
        ),
    )(depths, momenta, bed, active)


def solution(mesh):
    placed = (
        P(None, None, ("runs", "patch")),
        P(None, None, ("runs", "patch")),
        P(None, ("runs", "patch")),
        P(None, ("runs", "patch")),
    )
    return jax.shard_map(
        per_device,
        mesh=mesh,
        in_specs=placed,
        out_specs=(P(None, None, ("runs", "patch")), P(None, None, ("runs", "patch"))),
        check_vma=False,
    )
```

profile of v0, /device:TPU:0, one launch (start us, length us, event | category | flops | bytes accessed | tf_op | source)
XLA Modules:
  0.0 27.7 jit_solution(275932547950204433)
XLA Ops:
  1.3 0.0 copy-start
  1.3 0.9 %copy-done = f32[4,128,128]{2,1,0:T(8,128)S(1)} copy-done((f32[4,128,128]{2,1,0:T(8,128)S(1)}, f32[4,128,128]{2,1,0:T(8,128)}, u32[]{:S(2)}) %copy-start) | copy-done | bytes 262168
  2.2 0.0 copy-start.1
  2.2 0.9 %copy-done.1 = f32[2,128,128]{2,1,0:T(8,128)S(1)} copy-done((f32[2,128,128]{2,1,0:T(8,128)S(1)}, f32[2,128,128]{2,1,0:T(8,128)}, u32[]{:S(2)}) %copy-start.1) | copy-done | bytes 131096
  3.1 0.0 copy-start.2
  3.1 0.8 %copy-done.2 = f32[128,128]{1,0:T(8,128)S(1)} copy-done((f32[128,128]{1,0:T(8,128)S(1)}, f32[128,128]{1,0:T(8,128)}, u32[]{:S(2)}) %copy-start.2) | copy-done | bytes 65560
  4.0 22.3 %shard_map.59 = (f32[2,128,128]{2,1,0:T(8,128)S(1)}, f32[4,128,128]{2,1,0:T(8,128)S(1)}) custom-call(f32[2,128,128]{2,1,0:T(8,128)S(1)} %copy-done.1, f32[4,128,128]{2,1,0:T(8,128)S(1)} %copy-done, f32[128,128]{1,0:T(8,128)S(1)} %copy-done.2, s32[1,1]{1,0:T(1,128)S(6)} %copy.8.active), custom_call_target="tpu_custom_call" | custom-call | tf_op jit(solution)/shard_map/pallas_call | solution.py:309
  26.3 0.7 %copy.9 = f32[2,128,128]{2,1,0:T(8,128)} copy(f32[2,128,128]{2,1,0:T(8,128)S(1)} %get-tuple-element.4) | data formatting | bytes 262144
  27.0 0.7 %copy.10 = f32[4,128,128]{2,1,0:T(8,128)} copy(f32[4,128,128]{2,1,0:T(8,128)S(1)} %get-tuple-element.5) | data formatting | bytes 524288
Async XLA Ops:
  1.3 1.0 %copy-start = (f32[4,128,128]{2,1,0:T(8,128)S(1)}, f32[4,128,128]{2,1,0:T(8,128)}, u32[]{:S(2)}) copy-start(f32[4,128,128]{2,1,0:T(8,128)} %momenta.1) | copy-start | bytes 786436
  2.2 0.9 %copy-start.1 = (f32[2,128,128]{2,1,0:T(8,128)S(1)}, f32[2,128,128]{2,1,0:T(8,128)}, u32[]{:S(2)}) copy-start(f32[2,128,128]{2,1,0:T(8,128)} %depths.1) | copy-start | bytes 393220
  3.1 0.8 %copy-start.2 = (f32[128,128]{1,0:T(8,128)S(1)}, f32[128,128]{1,0:T(8,128)}, u32[]{:S(2)}) copy-start(f32[128,128]{1,0:T(8,128)} %bed.1) | copy-start | bytes 196612
where the time goes:
time: 27.9 us; the launch traced here: 27.7 us
  Pallas kernels  22.3 us (80%)
  local copies, waits for them, and re-layouts  4.05 us (15%)
  between operations  1.3 us (5%)
    pallas_call x1, Pallas kernels, per_device(): pl.pallas_call(functools.partial(kernel, count, rows), out_shape=(jax.Sha...  22.3 us
    unnamed x8, local copies, waits for them, and re-layouts  4.05 us

commit v1 on v0

v1 whole, which is shorter than its diff:
```python
import functools

import jax
import jax.numpy as jnp
from jax import lax
from jax.experimental import pallas as pl
from jax.experimental.pallas import tpu as pltpu
from jax.sharding import PartitionSpec as P

time_step = 0.04
solid_press = 0.6
fluid_press = 1.0
drag_coef = 0.5
friction_coef = 0.2
velocity_eps = 0.01
depth_eps = 0.0001
spread_eps = 1e-06
halo = 6
core_cols = 2 * halo
strip = 3 * halo
pair = 2 * strip
segments = 3
tiny = 1e-30
unroll = 9
step = 40
strip_groups = 8

MESH = pl.DeviceIdType.MESH


def recip(x):
    return pl.reciprocal(x, approx=True)


def lanes(x, shift):
    shift = shift % x.shape[-1]
    return x if shift == 0 else pltpu.roll(x, shift, 1)


def minmod(a, b):
    return jnp.maximum(jnp.minimum(a, b), jnp.minimum(jnp.maximum(a, b), 0.0))


def wave(depth, pressure):
    x = pressure * depth
    return jnp.maximum(x, 0.0) * lax.rsqrt(jnp.maximum(x, tiny))


def hll(left, right, pressure):
    hl, ml, tl = left
    hr, mr, tr = right
    hl2 = hl * hl
    hr2 = hr * hr
    ul = ml * hl * recip(hl2 + depth_eps)
    ur = mr * hr * recip(hr2 + depth_eps)
    cl = wave(hl, pressure)
    cr = wave(hr, pressure)
    low = jnp.minimum(jnp.minimum(ul - cl, ur - cr), 0.0)
    high = jnp.maximum(jnp.maximum(ul + cl, ur + cr), 0.0)
    r = time_step * recip(high - low + spread_eps)
    a = high * r
    b = low * r
    c = a * low
    al = a * ul - c
    br = b * ur - c
    fh = a * ml - b * mr + c * (hr - hl)
    fn = al * ml - br * mr + (0.5 * pressure) * (a * hl2 - b * hr2)
    ft = al * tl - br * tr
    return fh, fn, ft


def both_phases(left, right, offset):
    out = [None] * 6
    for phase, pressure in ((0, solid_press), (1, fluid_press)):
        ids = (phase, 2 + 2 * phase + offset, 3 + 2 * phase - offset)
        parts = hll([left[i] for i in ids], [right[i] for i in ids], pressure)
        for i, part in zip(ids, parts):
            out[i] = part
    return out


def row_states(src, at):
    lefts, rights = [], []
    for f in range(6):
        v = src[f, pl.ds(at, 8), :]
        below = src[f, pl.ds(at - 1, 8), :]
        above = src[f, pl.ds(at + 1, 8), :]
        s = 0.5 * minmod(v - below, above - v)
        lefts.append(v + s)
        rights.append(v - s)
    return lefts, rights


def tendency(v, br, bc):
    lefts, rights = [], []
    for f in range(6):
        h = 0.5 * v[f]
        d = h - lanes(h, 1)
        s = minmod(d, lanes(h, -1) - h)
        lefts.append(lanes(v[f] + s, 1))
        rights.append(v[f] - s)
    flux = both_phases(lefts, rights, 1)
    change = [lanes(x, -1) - x for x in flux]
    hs, hf = v[0], v[1]
    ws = hs * recip(hs * hs + depth_eps)
    wf = hf * recip(hf * hf + depth_eps)
    sr, sc, fr, fc = v[2] * ws, v[3] * ws, v[4] * wf, v[5] * wf
    drag = (time_step * drag_coef) * hs * hf * recip(jnp.abs(hs) + jnp.abs(hf) + depth_eps)
    rub = (time_step * friction_coef) * hs * lax.rsqrt(sr * sr + sc * sc + velocity_eps)
    dr = drag * (fr - sr)
    dc = drag * (fc - sc)
    ps = solid_press * hs
    pf = fluid_press * hf
    gains = [
        None,
        None,
        dr - ps * br - rub * sr,
        dc - ps * bc - rub * sc,
        dr + pf * br,
        dc + pf * bc,
    ]
    out = []
    for f in range(6):
        if f < 2:
            out.append(-change[f])
        elif f < 4:
            out.append(gains[f] - change[f])
        else:
            out.append(-gains[f] - change[f])
    return out


def run_stage(stage, buf, bed, at0, trips):
    src = buf.at[stage]
    dst = buf.at[stage + 1]
    old_part, new_part = ((0.0, 1.0), (0.75, 0.25), (1.0 / 3.0, 2.0 / 3.0))[stage]
    row = lax.broadcasted_iota(jnp.int32, (8, 128), 0)
    top = row == 0
    bottom = row == 7

    def faces(at, carried):
        lefts, rights = row_states(src, at)
        rolled = [pltpu.roll(x, 1, 0) for x in lefts]
        shifted = [jnp.where(top, a, b) for a, b in zip(carried, rolled)]
        return both_phases(shifted, rights, 0), rolled

    def one(at, carried, flux, rolled_flux):
        nxt, carried = faces(at + 8, carried)
        rolled_next = [pltpu.roll(x, 7, 0) for x in nxt]
        v = [src[f, pl.ds(at, 8), :] for f in range(6)]
        b = bed[pl.ds(at, 8), :]
        bed_r = (0.5 * time_step) * (bed[pl.ds(at + 1, 8), :] - bed[pl.ds(at - 1, 8), :])
        bed_c = (0.5 * time_step) * (lanes(b, -1) - lanes(b, 1))
        gain = tendency(v, bed_r, bed_c)
        for f in range(6):
            up = jnp.where(bottom, rolled_next[f], rolled_flux[f])
            new = v[f] + (gain[f] - (up - flux[f]))
            if stage:
                new = old_part * buf[0, f, pl.ds(at, 8), :] + new_part * new
            dst[f, pl.ds(at, 8), :] = new
        return carried, nxt, rolled_next

    def body(i, state):
        carried, flux, rolled_flux = state
        base = pl.multiple_of(at0 + i * (8 * unroll), 8)
        for u in range(unroll):
            carried, flux, rolled_flux = one(base + 8 * u, carried, flux, rolled_flux)
        return carried, flux, rolled_flux

    carried = [jnp.zeros((8, 128), jnp.float32)] * 6
    flux, carried = faces(at0, carried)
    rolled_flux = [pltpu.roll(x, 7, 0) for x in flux]
    lax.fori_loop(0, trips, body, (carried, flux, rolled_flux))


def kernel(count, rows, depths, momenta, bed_in, active, out_d, out_m,
           buf, bed, send, recv, load_sem, send_sem, recv_sem):
    me = lax.axis_index("patch")
    right, left = lax.rem(me + 1, count), lax.rem(me + count - 1, count)
    barrier = pltpu.get_barrier_semaphore()
    for other in (left, right):
        pl.semaphore_signal(barrier, inc=1, device_id={"patch": other}, device_id_type=MESH)

    end = 16 + rows
    loads = [
        pltpu.make_async_copy(depths, buf.at[0, 0:2, 16:end], load_sem.at[0]),
        pltpu.make_async_copy(momenta, buf.at[0, 2:6, 16:end], load_sem.at[1]),
        pltpu.make_async_copy(bed_in, bed.at[16:end], load_sem.at[2]),
    ]
    for load in loads:
        load.start()

    lane = lax.broadcasted_iota(jnp.int32, (8, 128), 1)
    strip0 = rows + 40
    fields = [buf.at[0, f] for f in range(6)] + [bed]
    for load in loads:
        load.wait()
    for x in fields:
        x[0:16, :] = jnp.broadcast_to(x[16:17, :], (16, 128))
        x[end : end + 24, :] = jnp.broadcast_to(x[end - 1 : end, :], (24, 128))

    def pack(q, carry):
        to_left = jnp.zeros((8, 128), jnp.float32)
        to_right = jnp.zeros((8, 128), jnp.float32)
        for f in range(7):
            for s in range(segments):
                v = fields[f][pl.ds(pl.multiple_of(8 + step * s + 8 * q, 8), 8), :]
                at = pair * s + halo * f if f < 6 else pair * segments + halo * s
                here = (lane >= at) & (lane < at + halo)
                to_left = jnp.where(here, lanes(v, at), to_left)
                to_right = jnp.where(here, lanes(v, at - (128 - halo)), to_right)
        rows_q = pl.ds(pl.multiple_of(8 * q, 8), 8)
        send[0, rows_q, :] = to_left
        send[1, rows_q, :] = to_right
        return carry

    lax.fori_loop(0, strip_groups, pack, 0, unroll=4)

    pl.semaphore_wait(barrier, 2)
    copies = []
    for i, other in ((0, left), (1, right)):
        copy = pltpu.make_async_remote_copy(
            src_ref=send.at[i],
            dst_ref=recv.at[i],
            send_sem=send_sem.at[i],
            recv_sem=recv_sem.at[i],
            device_id={"patch": other},
            device_id_type=MESH,
        )
        copy.start()
        copies.append(copy)

    def own_columns(q, carry):
        dest = pl.ds(pl.multiple_of(strip0 + 8 + 8 * q, 8), 8)
        for f in range(7):
            acc = jnp.zeros((8, 128), jnp.float32)
            for s in range(segments):
                v = fields[f][pl.ds(pl.multiple_of(8 + step * s + 8 * q, 8), 8), :]
                base = pair * s
                here = (lane >= base) & (lane < base + core_cols)
                acc = jnp.where(here, lanes(v, base - (128 - core_cols)), acc)
                base = base + strip + halo
                here = (lane >= base) & (lane < base + core_cols)
                acc = jnp.where(here, lanes(v, base), acc)
            fields[f][dest, :] = acc
        return carry

    lax.fori_loop(0, strip_groups, own_columns, 0, unroll=2)

    def within(begins, width):
        here = None
        for begin in begins:
            one = (lane >= begin) & (lane < begin + width)
            here = one if here is None else here | one
        return here

    starts = [pair * s for s in range(segments)]

    def halo_columns():
        sides = []
        for i, offset in ((0, core_cols), (1, strip)):
            sides.append((i, offset, within([b + offset for b in starts], halo)))
        for q in range(strip_groups):
            dest = pl.ds(strip0 + 8 + 8 * q, 8)
            got = [recv[i, 8 * q : 8 * q + 8, :] for i in range(2)]
            for f in range(7):
                acc = fields[f][dest, :]
                for i, offset, here in sides:
                    if f < 6:
                        acc = jnp.where(here, lanes(got[i], offset - halo * f), acc)
                    else:
                        for s in range(segments):
                            begin = pair * s + offset
                            moved = lanes(got[i], begin - (pair * segments + halo * s))
                            acc = jnp.where(within([begin], halo), moved, acc)
                fields[f][dest, :] = acc

    def tile(t, carry):
        @pl.when(t == 1)
        def _():
            for copy in copies:
                copy.wait()
            halo_columns()
            for x in fields:
                x[strip0 : strip0 + 8, :] = x[strip0 + 8 : strip0 + 16, :]
                x[strip0 + 72 : strip0 + 96, :] = x[strip0 + 48 : strip0 + 72, :]

        at0 = pl.multiple_of(8 + t * strip0, 8)
        trips = jnp.where(t == 0, (rows // 8 + 1 + unroll) // unroll, (strip_groups - 1 + unroll) // unroll)

        def stage_body(stage, carry):
            run_stage(stage, buf, bed, at0, trips)
            return carry

        for stage in range(3):
            run_stage(stage, buf, bed, at0, trips)
        return carry

    lax.fori_loop(0, 2, tile, 0)

    live = jnp.broadcast_to(active[...], (8, 128)) > 0
    left_edge = lane < halo
    right_edge = lane >= 128 - halo

    def merge(s, begin):
        for q in range(begin, strip_groups):
            row_at = 8 * q + step * s - 16
            for f in range(6):
                e = buf[3, f, strip0 + 8 * q : strip0 + 8 * q + 8, :]
                new = buf[3, f, row_at + 16 : row_at + 24, :]
                new = jnp.where(left_edge, lanes(e, -(pair * s + strip + halo)), new)
                new = jnp.where(right_edge, lanes(e, 128 - halo - (pair * s + halo)), new)
                new = jnp.where(live, new, buf[0, f, row_at + 16 : row_at + 24, :])
                if f < 2:
                    out_d[f, row_at : row_at + 8, :] = new
                else:
                    out_m[f - 2, row_at : row_at + 8, :] = new

    merge(0, 2)
    merge(1, 3)
    merge(2, 3)


def per_device(depths, momenta, bed, active):
    rows, cols = bed.shape
    count = lax.axis_size("patch")
    tall = rows + 40 + 96
    f32 = jnp.float32
    vmem = pl.BlockSpec(memory_space=pltpu.VMEM)
    hbm = pl.BlockSpec(memory_space=pltpu.HBM)
    return pl.pallas_call(
        functools.partial(kernel, count, rows),
        out_shape=(
            jax.ShapeDtypeStruct(depths.shape, f32),
            jax.ShapeDtypeStruct(momenta.shape, f32),
        ),
        in_specs=[hbm, hbm, hbm, vmem],
        out_specs=(vmem, vmem),
        scratch_shapes=[
            pltpu.VMEM((4, 6, tall, cols), f32),
            pltpu.VMEM((tall, cols), f32),
            pltpu.VMEM((2, 64, cols), f32),
            pltpu.VMEM((2, 64, cols), f32),
            pltpu.SemaphoreType.DMA((3,)),
            pltpu.SemaphoreType.DMA((2,)),
            pltpu.SemaphoreType.DMA((2,)),
        ],
        compiler_params=pltpu.CompilerParams(
            collective_id=0, has_side_effects=True, vmem_limit_bytes=32 * 1024 * 1024
        ),
    )(depths, momenta, bed, active)


def solution(mesh):
    placed = (
        P(None, None, ("runs", "patch")),
        P(None, None, ("runs", "patch")),
        P(None, ("runs", "patch")),
        P(None, ("runs", "patch")),
    )
    return jax.shard_map(
        per_device,
        mesh=mesh,
        in_specs=placed,
        out_specs=(P(None, None, ("runs", "patch")), P(None, None, ("runs", "patch"))),
        check_vma=False,
    )
```

time: 27.9 us -> 19.7 us (0.71)
  Pallas kernels: 22.3 us -> 14.2 us
    pallas_call x1, Pallas kernels: 22.3 us -> 14.2 us  [per_device(): pl.pallas_call(functools.partial(kernel, count, rows), out_shape=(jax.Sha...]
where the time goes in v1:
time: 19.7 us; the launch traced here: 19.5 us
  Pallas kernels  14.2 us (72%)
  local copies, waits for them, and re-layouts  4.05 us (21%)
  between operations  1.3 us (7%)
    pallas_call x1, Pallas kernels, per_device(): pl.pallas_call(functools.partial(kernel, count, rows), out_shape=(jax.Sha...  14.2 us
    unnamed x8, local copies, waits for them, and re-layouts  4.05 us

profile of v1, /device:TPU:0, one launch (start us, length us, event | category | flops | bytes accessed | tf_op | source)
XLA Modules:
  0.0 19.5 jit_solution(3259952826807104551)
XLA Ops:
  1.3 0.0 copy-start
  1.3 0.9 %copy-done = f32[4,128,128]{2,1,0:T(8,128)S(1)} copy-done((f32[4,128,128]{2,1,0:T(8,128)S(1)}, f32[4,128,128]{2,1,0:T(8,128)}, u32[]{:S(2)}) %copy-start) | copy-done | bytes 262168
  2.2 0.0 copy-start.1
  2.2 0.9 %copy-done.1 = f32[2,128,128]{2,1,0:T(8,128)S(1)} copy-done((f32[2,128,128]{2,1,0:T(8,128)S(1)}, f32[2,128,128]{2,1,0:T(8,128)}, u32[]{:S(2)}) %copy-start.1) | copy-done | bytes 131096
  3.1 0.0 copy-start.2
  3.1 0.8 %copy-done.2 = f32[128,128]{1,0:T(8,128)S(1)} copy-done((f32[128,128]{1,0:T(8,128)S(1)}, f32[128,128]{1,0:T(8,128)}, u32[]{:S(2)}) %copy-start.2) | copy-done | bytes 65560
  4.0 14.2 %shard_map.59 = (f32[2,128,128]{2,1,0:T(8,128)S(1)}, f32[4,128,128]{2,1,0:T(8,128)S(1)}) custom-call(f32[2,128,128]{2,1,0:T(8,128)S(1)} %copy-done.1, f32[4,128,128]{2,1,0:T(8,128)S(1)} %copy-done, f32[128,128]{1,0:T(8,128)S(1)} %copy-done.2, s32[1,1]{1,0:T(1,128)S(6)} %copy.8.active), custom_call_target="tpu_custom_call" | custom-call | tf_op jit(solution)/shard_map/pallas_call | solution.py:331
  18.2 0.7 %copy.9 = f32[2,128,128]{2,1,0:T(8,128)} copy(f32[2,128,128]{2,1,0:T(8,128)S(1)} %get-tuple-element.4) | data formatting | bytes 262144
  18.8 0.7 %copy.10 = f32[4,128,128]{2,1,0:T(8,128)} copy(f32[4,128,128]{2,1,0:T(8,128)S(1)} %get-tuple-element.5) | data formatting | bytes 524288
Async XLA Ops:
  1.3 1.0 %copy-start = (f32[4,128,128]{2,1,0:T(8,128)S(1)}, f32[4,128,128]{2,1,0:T(8,128)}, u32[]{:S(2)}) copy-start(f32[4,128,128]{2,1,0:T(8,128)} %momenta.1) | copy-start | bytes 786436
  2.2 0.9 %copy-start.1 = (f32[2,128,128]{2,1,0:T(8,128)S(1)}, f32[2,128,128]{2,1,0:T(8,128)}, u32[]{:S(2)}) copy-start(f32[2,128,128]{2,1,0:T(8,128)} %depths.1) | copy-start | bytes 393220
  3.1 0.8 %copy-start.2 = (f32[128,128]{1,0:T(8,128)S(1)}, f32[128,128]{1,0:T(8,128)}, u32[]{:S(2)}) copy-start(f32[128,128]{1,0:T(8,128)} %bed_in.1) | copy-start | bytes 196612

commit v2 on v1

--- a/solution.py
+++ b/solution.py
@@ -24,6 +24,7 @@
 unroll = 9
 step = 40
 strip_groups = 8
+send_after = 0
 
 MESH = pl.DeviceIdType.MESH
 
@@ -216,10 +217,8 @@
 
     lax.fori_loop(0, strip_groups, pack, 0, unroll=4)
 
-    pl.semaphore_wait(barrier, 2)
-    copies = []
-    for i, other in ((0, left), (1, right)):
-        copy = pltpu.make_async_remote_copy(
+    copies = [
+        pltpu.make_async_remote_copy(
             src_ref=send.at[i],
             dst_ref=recv.at[i],
             send_sem=send_sem.at[i],
@@ -227,8 +226,8 @@
             device_id={"patch": other},
             device_id_type=MESH,
         )
-        copy.start()
-        copies.append(copy)
+        for i, other in ((0, left), (1, right))
+    ]
 
     def own_columns(q, carry):
         dest = pl.ds(pl.multiple_of(strip0 + 8 + 8 * q, 8), 8)
@@ -288,12 +287,16 @@
         at0 = pl.multiple_of(8 + t * strip0, 8)
         trips = jnp.where(t == 0, (rows // 8 + 1 + unroll) // unroll, (strip_groups - 1 + unroll) // unroll)
 
-        def stage_body(stage, carry):
-            run_stage(stage, buf, bed, at0, trips)
-            return carry
-
         for stage in range(3):
             run_stage(stage, buf, bed, at0, trips)
+            if stage == send_after:
+
+                @pl.when(t == 0)
+                def _():
+                    pl.semaphore_wait(barrier, 2)
+                    for copy in copies:
+                        copy.start()
+
         return carry
 
     lax.fori_loop(0, 2, tile, 0)

time: 19.7 us -> 18.7 us (0.949)
  Pallas kernels: 14.2 us -> 13.1 us
    pallas_call x1, Pallas kernels: 14.2 us -> 13.1 us  [per_device(): pl.pallas_call(functools.partial(kernel, count, rows), out_shape=(jax.Sha...]
where the time goes in v2:
time: 18.7 us; the launch traced here: 18.4 us
  Pallas kernels  13.1 us (70%)
  local copies, waits for them, and re-layouts  4.05 us (22%)
  between operations  1.3 us (7%)
    pallas_call x1, Pallas kernels, per_device(): pl.pallas_call(functools.partial(kernel, count, rows), out_shape=(jax.Sha...  13.1 us
    unnamed x8, local copies, waits for them, and re-layouts  4.05 us

profile of v2, /device:TPU:0, one launch (start us, length us, event | category | flops | bytes accessed | tf_op | source)
XLA Modules:
  0.0 18.4 jit_solution(12170556194177449929)
XLA Ops:
  1.3 0.0 copy-start
  1.3 0.9 %copy-done = f32[4,128,128]{2,1,0:T(8,128)S(1)} copy-done((f32[4,128,128]{2,1,0:T(8,128)S(1)}, f32[4,128,128]{2,1,0:T(8,128)}, u32[]{:S(2)}) %copy-start) | copy-done | bytes 262168
  2.2 0.0 copy-start.1
  2.2 0.9 %copy-done.1 = f32[2,128,128]{2,1,0:T(8,128)S(1)} copy-done((f32[2,128,128]{2,1,0:T(8,128)S(1)}, f32[2,128,128]{2,1,0:T(8,128)}, u32[]{:S(2)}) %copy-start.1) | copy-done | bytes 131096
  3.1 0.0 copy-start.2
  3.1 0.8 %copy-done.2 = f32[128,128]{1,0:T(8,128)S(1)} copy-done((f32[128,128]{1,0:T(8,128)S(1)}, f32[128,128]{1,0:T(8,128)}, u32[]{:S(2)}) %copy-start.2) | copy-done | bytes 65560
  4.0 13.1 %shard_map.59 = (f32[2,128,128]{2,1,0:T(8,128)S(1)}, f32[4,128,128]{2,1,0:T(8,128)S(1)}) custom-call(f32[2,128,128]{2,1,0:T(8,128)S(1)} %copy-done.1, f32[4,128,128]{2,1,0:T(8,128)S(1)} %copy-done, f32[128,128]{1,0:T(8,128)S(1)} %copy-done.2, s32[1,1]{1,0:T(1,128)S(6)} %copy.8.active), custom_call_target="tpu_custom_call" | custom-call | tf_op jit(solution)/shard_map/pallas_call | solution.py:334
  17.1 0.7 %copy.9 = f32[2,128,128]{2,1,0:T(8,128)} copy(f32[2,128,128]{2,1,0:T(8,128)S(1)} %get-tuple-element.4) | data formatting | bytes 262144
  17.7 0.7 %copy.10 = f32[4,128,128]{2,1,0:T(8,128)} copy(f32[4,128,128]{2,1,0:T(8,128)S(1)} %get-tuple-element.5) | data formatting | bytes 524288
Async XLA Ops:
  1.3 1.0 %copy-start = (f32[4,128,128]{2,1,0:T(8,128)S(1)}, f32[4,128,128]{2,1,0:T(8,128)}, u32[]{:S(2)}) copy-start(f32[4,128,128]{2,1,0:T(8,128)} %momenta.1) | copy-start | bytes 786436
  2.2 0.9 %copy-start.1 = (f32[2,128,128]{2,1,0:T(8,128)S(1)}, f32[2,128,128]{2,1,0:T(8,128)}, u32[]{:S(2)}) copy-start(f32[2,128,128]{2,1,0:T(8,128)} %depths.1) | copy-start | bytes 393220
  3.1 0.8 %copy-start.2 = (f32[128,128]{1,0:T(8,128)S(1)}, f32[128,128]{1,0:T(8,128)}, u32[]{:S(2)}) copy-start(f32[128,128]{1,0:T(8,128)} %bed_in.1) | copy-start | bytes 196612
